TPU v7x, 128 devices: a whole 4x4x4 slice. The times are simulated.
128 devices in a mesh: ia: 2 (over z_hi), ja: 8 (over x, core), ka: 8 (over y, z_lo).
Axes of the slice: x: 4, y: 4, z: 4 (z_hi: 2, z_lo: 2; z = z_hi * 2 + z_lo), core: 2. Of those that a mesh axis runs over, the one named last changes fastest.
Arguments:
- hidden_act: bfloat16 [768, 26624], P(('ia', 'ka'), 'ja'), may hold values from -6 to 6
- w_down: bfloat16 [26624, 16384], P('ja', ('ia', 'ka')), may hold values from -0.0390625 to 0.0390625
- w_out: bfloat16 [16384, 16384], P(('ia', 'ka'), 'ja'), may hold values from -0.046875 to 0.046875
- head_grad: bfloat16 [768, 16384], P(('ia', 'ka'), 'ja'), may hold values from -6 to 6
- token_ratio: float32 [768], P(('ia', 'ka')), may hold values from -4 to 4
- pair_slot: int32 [768], P(('ia', 'ka')), may hold values from 0 to 15
- segment_id: int32 [768], P(('ia', 'ka')), may hold values from 0 to 191, never falling along the last dimension, each value on 1 to 16 neighbouring positions
Outputs:
- projected: bfloat16 [768, 16384], P(('ia', 'ka'), 'ja')
- grad_hidden: bfloat16 [768, 26624], P(('ia', 'ka'), 'ja')
- grad_down: bfloat16 [26624, 16384], P('ja', ('ia', 'ka'))
- grad_out: bfloat16 [16384, 16384], P(('ia', 'ka'), 'ja')
All inputs are finite; a program needn't handle non-finite values.
Results may differ from a plain program's by a relative error of at most 0.0058.
Values may be sent and summed in bfloat16 or wider, within the bound.
A program may use at most 128 MiB of HBM per device.

v0:
```python
import jax
import jax.numpy as jnp
from jax import lax
from jax.sharding import PartitionSpec as P

PAIRS = 8


beta_scale = 0.5


def gather_rows(block):
    return lax.all_gather(block, ("ia", "ka"), axis=0, tiled=True)


def scatter_rows(term, local_rows):
    return lax.psum_scatter(
        term(jnp.int32(0), local_rows * lax.axis_size(("ia", "ka"))),
        ("ia", "ka"),
        scatter_dimension=0,
        tiled=True,
    )


def summed_middle(term, total_rows):
    shares = lax.psum_scatter(
        term(jnp.int32(0), total_rows // lax.axis_size("ja") * lax.axis_size("ja")),
        "ja",
        scatter_dimension=0,
        tiled=True,
    ).astype(jnp.bfloat16)
    return lax.all_gather(shares, "ja", axis=0, tiled=True)


def contract_last(left, right):
    return lax.dot_general(
        left, right, (((1,), (1,)), ((), ())), preferred_element_type=jnp.float32
    )


def contract_first(left, right):
    return lax.dot_general(
        left, right, (((0,), (0,)), ((), ())), preferred_element_type=jnp.float32
    )


def local(hidden_act, w_down, w_out, head_grad, token_ratio, pair_slot, segment_id):
    local_rows = hidden_act.shape[0]
    total_rows = local_rows * lax.axis_size("ia") * lax.axis_size("ka")
    full_hidden = gather_rows(hidden_act)

    def down_term(start, count):
        return jnp.dot(full_hidden, w_down, preferred_element_type=jnp.float32)

    down_full = summed_middle(down_term, total_rows)

    def out_term(start, count):
        return jnp.dot(down_full, w_out, preferred_element_type=jnp.float32)

    projected = scatter_rows(out_term, local_rows).astype(jnp.bfloat16)
    masked = (segment_id % 2).astype(jnp.float32)
    signed = masked * (1 - 2 * (pair_slot % 2)).astype(jnp.float32)
    onehot = ((pair_slot // 2)[:, None] == jnp.arange(PAIRS, dtype=jnp.int32)[None, :]).astype(
        jnp.float32
    )
    local_margin = jnp.dot(signed * token_ratio, onehot, precision=lax.Precision.HIGHEST)
    margin = lax.psum(local_margin, ("ia", "ka"))
    pair_weight = -beta_scale * jax.nn.sigmoid(-beta_scale * margin)
    coef = jnp.dot(onehot, pair_weight, precision=lax.Precision.HIGHEST) * signed
    cotangent = (coef[:, None] * head_grad.astype(jnp.float32)).astype(jnp.bfloat16)
    full_cotangent = gather_rows(cotangent)

    def back_term(start, count):
        return contract_last(full_cotangent, w_out)

    grad_mid = summed_middle(back_term, total_rows)
    grad_out = contract_first(down_full, full_cotangent).astype(jnp.bfloat16)

    def hidden_term(start, count):
        return contract_last(grad_mid, w_down)

    grad_hidden = scatter_rows(hidden_term, local_rows).astype(jnp.bfloat16)
    grad_down = contract_first(full_hidden, grad_mid).astype(jnp.bfloat16)
    return (projected, grad_hidden, grad_down, grad_out)


def solution(mesh):
    placed = (
        P(("ia", "ka"), "ja"),
        P("ja", ("ia", "ka")),
        P(("ia", "ka"), "ja"),
        P(("ia", "ka"), "ja"),
        P(("ia", "ka")),
        P(("ia", "ka")),
        P(("ia", "ka")),
    )
    return jax.shard_map(
        local,
        mesh=mesh,
        in_specs=placed,
        out_specs=(
            P(("ia", "ka"), "ja"),
            P(("ia", "ka"), "ja"),
            P("ja", ("ia", "ka")),
            P(("ia", "ka"), "ja"),
        ),
        check_vma=False,
    )
```

profile of v0, /device:TPU:1, one launch (start us, length us, event | category | flops | bytes accessed | tf_op | source)
XLA Modules:
  0.0 707.1 jit_solution(12141324303579329130)
XLA Ops:
  7.2 0.7 all-gather.5.cloned.1.call-update
  7.9 0.7 and_select_fusion.2
  8.6 0.7 fusion.5
  9.3 0.8 convolution_bitcast_fusion.1
  10.1 37.1 %psum.7 = f32[8]{0:T(128)S(1)} all-reduce(f32[8]{0:T(128)S(1)} %convolution_bitcast_fusion.1), channel_id=1, replica_groups=mesh['ia'=2,'ja'=8,'ka'=8] {'ia','ka'}, use_global_device_ids=true, to_apply=%region_2.3 | all-reduce | flops 8 | bytes 64 | tf_op jit(solution)/shard_map/psum | solution.py:67
  47.2 0.2 fusion.1
  47.4 1.7 multiply_convert_fusion
  49.1 0.0 reduce-scatter.5.cloned.1.call-start
  49.2 75.3 %all-gather.5.cloned.1.call-done = bf16[768,3328]{1,0:T(8,128)(2,1)} async-done(((bf16[48,3328]{1,0:T(8,128)(2,1)}), bf16[768,3328]{1,0:T(8,128)(2,1)}) %all-gather.5.cloned.1.call-update) | async-done | bytes 5111824 | tf_op jit(solution)/shard_map/all_gather | solution.py:13
  124.5 10.2 %fusion.19 = f32[768,1024]{1,0:T(8,128)} fusion(bf16[768,3328]{1,0:T(8,128)(2,1)} %all-gather.5.cloned.1.call-done, bf16[3328,1024]{1,0:T(8,128)(2,1)} %param.8), kind=kOutput, calls=%fused_computation.35 | convolution fusion | flops 5234491392 | bytes 15073280 | tf_op jit(solution)/shard_map/dot_general | solution.py:53
  134.8 0.0 reduce-scatter.9.cloned.1.call-start
  134.8 71.2 %all-gather.9.cloned.1.call-done = bf16[768,2048]{1,0:T(8,128)(2,1)} async-done(((bf16[48,2048]{1,0:T(8,128)(2,1)}), bf16[768,2048]{1,0:T(8,128)(2,1)}) %all-gather.9.cloned.1.call-update) | async-done | bytes 3145744 | tf_op jit(solution)/shard_map/all_gather | solution.py:13
  206.1 8.2 %fusion.21 = f32[768,1024]{1,0:T(8,128)} fusion(bf16[768,2048]{1,0:T(8,128)(2,1)} %all-gather.9.cloned.1.call-done, bf16[1024,2048]{1,0:T(8,128)(2,1)} %param.9), kind=kOutput, calls=%fused_computation.37 | convolution fusion | flops 3221225472 | bytes 10485760 | tf_op jit(solution)/shard_map/dot_general | solution.py:36
  214.4 0.0 all-gather.7.cloned.1.call-start
  214.4 32.5 %reduce-scatter.5.cloned.1.call-done = f32[96,1024]{1,0:T(8,128)} async-done(((f32[768,1024]{1,0:T(8,128)}), f32[96,1024]{1,0:T(8,128)}) %reduce-scatter.5.cloned.1.call-update) | async-done | bytes 393232 | tf_op jit(solution)/shard_map/reduce_scatter | solution.py:26
  246.9 1.7 convert_element_type.34
  248.6 0.0 all-gather.11.cloned.1.call-start
  248.7 35.6 %reduce-scatter.9.cloned.1.call-done = f32[96,1024]{1,0:T(8,128)} async-done(((f32[768,1024]{1,0:T(8,128)}), f32[96,1024]{1,0:T(8,128)}) %reduce-scatter.9.cloned.1.call-update) | async-done | bytes 393232 | tf_op jit(solution)/shard_map/reduce_scatter | solution.py:26
  284.3 1.7 convert_element_type.40
  286.1 27.1 %all-gather.7.cloned.1.call-done = bf16[768,1024]{1,0:T(8,128)(2,1)} async-done(((bf16[96,1024]{1,0:T(8,128)(2,1)}), bf16[768,1024]{1,0:T(8,128)(2,1)}) %all-gather.7.cloned.1.call-update) | async-done | bytes 1572880 | tf_op jit(solution)/shard_map/all_gather | solution.py:32
  313.2 8.7 %fusion.20 = f32[768,2048]{1,0:T(8,128)} fusion(bf16[768,1024]{1,0:T(8,128)(2,1)} %all-gather.7.cloned.1.call-done, bf16[1024,2048]{1,0:T(8,128)(2,1)} %param.9), kind=kOutput, calls=%fused_computation.36 | convolution fusion | flops 3221225472 | bytes 12058624 | tf_op jit(solution)/shard_map/dot_general | solution.py:58
  321.9 0.2 reduce-scatter.11.cloned.1.call-start
  322.2 17.9 %all-gather.11.cloned.1.call-done = bf16[768,1024]{1,0:T(8,128)(2,1)} async-done(((bf16[96,1024]{1,0:T(8,128)(2,1)}), bf16[768,1024]{1,0:T(8,128)(2,1)}) %all-gather.11.cloned.1.call-update) | async-done | bytes 1572880 | tf_op jit(solution)/shard_map/all_gather | solution.py:32
  340.0 11.2 %fusion.22 = f32[768,3328]{1,0:T(8,128)} fusion(bf16[768,1024]{1,0:T(8,128)(2,1)} %all-gather.11.cloned.1.call-done, bf16[3328,1024]{1,0:T(8,128)(2,1)} %param.8), kind=kOutput, calls=%fused_computation.38 | convolution fusion | flops 5234491392 | bytes 18612224 | tf_op jit(solution)/shard_map/dot_general | solution.py:36
  351.2 1.4 copy-done.1
  352.6 9.9 %fusion = bf16[3328,1024]{0,1:T(8,128)(2,1)} fusion(bf16[768,1024]{1,0:T(8,128)(2,1)S(1)} %copy-done.1, bf16[768,3328]{1,0:T(8,128)(2,1)} %all-gather.5.cloned.1.call-done), kind=kOutput, calls=%fused_computation.1 | convolution fusion | flops 5237899264 | bytes 13500416 | tf_op jit(solution)/shard_map/dot_general | solution.py:42
  362.5 10.1 %copy.11 = bf16[3328,1024]{1,0:T(8,128)(2,1)} copy(bf16[3328,1024]{0,1:T(8,128)(2,1)} %fusion) | data formatting | bytes 13631488
  372.7 6.4 convolution_convert_fusion.1
  379.1 101.0 %reduce-scatter.7.cloned.1.call-done = f32[48,2048]{1,0:T(8,128)} async-done(((f32[768,2048]{1,0:T(8,128)}), f32[48,2048]{1,0:T(8,128)}) %reduce-scatter.7.cloned.1.call-update) | async-done | bytes 393232 | tf_op jit(solution)/shard_map/reduce_scatter | solution.py:17
  480.1 1.7 convert_element_type.35
  481.8 216.6 %reduce-scatter.11.cloned.1.call-done = f32[48,3328]{1,0:T(8,128)} async-done(((f32[768,3328]{1,0:T(8,128)}), f32[48,3328]{1,0:T(8,128)}) %reduce-scatter.11.cloned.1.call-update) | async-done | bytes 638992 | tf_op jit(solution)/shard_map/reduce_scatter | solution.py:17
  698.4 1.8 convert_element_type.41
  (13 shorter events, 0.2 us)
Async XLA Ops:
  7.2 117.4 %all-gather.5.cloned.1.call-start = ((), (), s32[]{:S(2)}) async-start(), calls=%async_computation.4 | async-start | bytes 5431296 | tf_op jit(solution)/shard_map/all_gather | solution.py:13
  7.9 198.2 %all-gather.9.cloned.1.call-start = ((), (), s32[]{:S(2)}) async-start(), calls=%async_computation.8 | async-start | bytes 3342336 | tf_op jit(solution)/shard_map/all_gather | solution.py:13
  49.1 197.8 %reduce-scatter.5.cloned.1.call-start = ((), (), s32[]{:S(2)}) async-start(), calls=%async_computation.5 | async-start | bytes 3538944 | tf_op jit(solution)/shard_map/reduce_scatter | solution.py:26
  134.8 149.6 %reduce-scatter.9.cloned.1.call-start = ((), (), s32[]{:S(2)}) async-start(), calls=%async_computation.9 | async-start | bytes 3538944 | tf_op jit(solution)/shard_map/reduce_scatter | solution.py:26
  214.4 98.8 %all-gather.7.cloned.1.call-start = ((), (), s32[]{:S(2)}) async-start(), calls=%async_computation.6 | async-start | bytes 1769472 | tf_op jit(solution)/shard_map/all_gather | solution.py:32
  248.6 91.4 %all-gather.11.cloned.1.call-start = ((), (), s32[]{:S(2)}) async-start(), calls=%async_computation.10 | async-start | bytes 1769472 | tf_op jit(solution)/shard_map/all_gather | solution.py:32
  286.1 194.0 %reduce-scatter.7.cloned.1.call-start = ((), (), s32[]{:S(2)}) async-start(), calls=%async_computation.7 | async-start | bytes 6684672 | tf_op jit(solution)/shard_map/reduce_scatter | solution.py:17
  321.9 376.5 %reduce-scatter.11.cloned.1.call-start = ((), (), s32[]{:S(2)}) async-start(), calls=%async_computation.11 | async-start | bytes 10862592 | tf_op jit(solution)/shard_map/reduce_scatter | solution.py:17
  351.2 1.4 copy-start.1
  362.5 10.1 %copy-start = (bf16[768,2048]{1,0:T(8,128)(2,1)S(1)}, bf16[768,2048]{1,0:T(8,128)(2,1)}, u32[]{:S(2)}) copy-start(bf16[768,2048]{1,0:T(8,128)(2,1)} %all-gather.9.cloned.1.call-done) | copy-start | bytes 9437188
Sparse Core Ops, SparseCore 0:
  9.6 114.8 all-gather.4
  126.7 79.2 all-gather.8
  209.1 37.8 reduce-scatter.4
  249.8 34.5 reduce-scatter.8
  286.4 26.6 all-gather.6
  315.3 24.6 all-gather.10
  342.4 137.6 reduce-scatter.6
  482.5 215.8 reduce-scatter.10
where the time goes:
time: 709 us; the launch traced here: 707 us
  waiting for transfers between devices  578 us (82%)
  matrix products  55.8 us (8%)
  blocking collectives  37.1 us (5%)
  between operations  14.1 us (2%)
  local copies, waits for them, and re-layouts  11.5 us (2%)
  other arithmetic  10 us (1%)
    reduce_scatter x2, waiting for transfers between devices, scatter_rows(): lax.psum_scatter(term(jnp.int32(0), local_rows * lax.axis_size(('ia', 'ka...  318 us
    all_gather x2, waiting for transfers between devices, gather_rows(): return lax.all_gather(block, ('ia', 'ka'), axis=0, tiled=True)  147 us
    reduce_scatter x2, waiting for transfers between devices, summed_middle(): lax.psum_scatter(term(jnp.int32(0), total_rows // lax.axis_size('ja') * l...  68.2 us
    all_gather x2, waiting for transfers between devices, summed_middle(): return lax.all_gather(shares, 'ja', axis=0, tiled=True)  44.9 us
    psum x1, blocking collectives, local(): margin = lax.psum(local_margin, ('ia', 'ka'))  37.1 us
    dot_general x2, matrix products, contract_last(): lax.dot_general(left, right, (((1,), (1,)), ((), ())), preferred_element_...  19.4 us
    dot_general x2, matrix products, contract_first(): lax.dot_general(left, right, (((0,), (0,)), ((), ())), preferred_element_...  16.3 us
  transfers between devices with their start and end apart: 8, of which 8 were waited for; matrix products, arithmetic and copies ran while one was open for 10% of the time, Pallas kernels for 0%

commit v1 on v0

v1 whole, which is shorter than its diff:
```python
import functools

import jax
import jax.numpy as jnp
from jax import lax
from jax.experimental import pallas as pl
from jax.experimental.pallas import tpu as pltpu
from jax.sharding import PartitionSpec as P

PAIRS = 8
MESH = pl.DeviceIdType.MESH
BF = jnp.bfloat16
F32 = jnp.float32

beta_scale = 0.5


def dot_nt(a, b):
    return lax.dot_general(a, b, (((1,), (1,)), ((), ())), preferred_element_type=F32)


def dot_nn(a, b):
    return lax.dot_general(a, b, (((1,), (0,)), ((), ())), preferred_element_type=F32)


def kernel(
    rows, tile_ref, hid_ref, wd_ref, wo_ref, hg_ref,
    proj_ref, gh_ref, gd_ref, go_ref,
    wd, wo, hid, hg, cot, tiles,
    sib_out, sib_in, part, xout, xin, gm, dn,
    g_out, g_in, g_acc, g_out2, g_in2, g_fin,
    p_out, p_in, p_acc, p_out2, p_in2, p_fin,
    stage, ssem, rsem, lsem, osem,
):
    ia, ja, ka = lax.axis_index("ia"), lax.axis_index("ja"), lax.axis_index("ka")
    z, y, x, core = ia * 2 + ka % 2, ka // 2, ja // 2, ja % 2

    def peer(dx=0, dc=0, dy=0, dz=0):
        pz, py, px, pc = (z + dz) % 4, (y + dy) % 4, (x + dx) % 4, (core + dc) % 2
        return (pz // 2, px * 2 + pc, py * 2 + pz % 2)

    count = [0]
    sent = []

    def send(src, dst, **where):
        i = count[0]
        count[0] += 1
        copy = pltpu.make_async_remote_copy(
            src, dst, ssem.at[i], rsem.at[i], device_id=peer(**where), device_id_type=MESH
        )
        copy.start()
        sent.append(copy)
        return copy

    def finish(copies):
        for copy in copies:
            copy.wait_send()
            sent[:] = [other for other in sent if other is not copy]

    def arrive(copies):
        for copy in copies:
            copy.wait_recv()

    near = (2, 1, 3)

    loads = [
        pltpu.make_async_copy(hg_ref, hg.at[0, 0], lsem.at[0]),
        pltpu.make_async_copy(hid_ref, hid.at[0, 0], lsem.at[1]),
        pltpu.make_async_copy(tile_ref, tiles.at[0, 0], lsem.at[2]),
        pltpu.make_async_copy(wo_ref, wo, lsem.at[3]),
        pltpu.make_async_copy(wd_ref, wd, lsem.at[4]),
    ]
    for load in loads:
        load.start()

    barrier = pltpu.get_barrier_semaphore()
    peers = [dict(dc=1)] + [{a: d} for a in ("dx", "dy", "dz") for d in near]
    for where in peers:
        pl.semaphore_signal(barrier, inc=1, device_id=peer(**where), device_id_type=MESH)
    pl.semaphore_wait(barrier, len(peers))
    for load in loads[:3]:
        load.wait()

    def gather_first(full):
        half = full.shape[3] // 2
        lo, hi = pl.ds(0, half), pl.ds(half, half)
        first = [
            send(full.at[0, 0, :, lo], full.at[0, (4 - d) % 4, :, lo], dy=d) for d in near
        ]
        other = [
            send(full.at[0, 0, :, hi], full.at[(4 - d) % 4, 0, :, hi], dz=d) for d in near
        ]
        return first, other

    def gather_second(full, first, other):
        half = full.shape[3] // 2
        lo, hi = pl.ds(0, half), pl.ds(half, half)
        arrive(first)
        copies = [
            send(full.at[0, :, :, lo], full.at[(4 - d) % 4, :, :, lo], dz=d) for d in near
        ]
        arrive(other)
        return copies + [
            send(full.at[:, 0, :, hi], full.at[:, (4 - d) % 4, :, hi], dy=d) for d in near
        ]

    tile_first = [send(tiles.at[0, 0], tiles.at[0, (4 - d) % 4], dy=d) for d in near]
    hg_first = gather_first(hg)
    hid_first = gather_first(hid)
    arrive(tile_first)
    tile_second = [send(tiles.at[0], tiles.at[(4 - d) % 4], dz=d) for d in near]
    hg_second = gather_second(hg, *hg_first)
    hid_second = gather_second(hid, *hid_first)

    arrive(tile_second)
    margin = jnp.sum(tiles[:, :, 0:rows, :], axis=(0, 1, 2))[None, :]
    weight = -beta_scale * jax.nn.sigmoid(-beta_scale * margin)

    arrive(hg_second)

    def scale(i, _):
        coef = jnp.sum(tiles[i // 4, i % 4, rows:, :] * weight, axis=1, keepdims=True)
        cot[i // 4, i % 4] = (coef * hg[i // 4, i % 4].astype(F32)).astype(BF)
        return 0

    lax.fori_loop(0, 16, scale, 0)

    tokens = 16 * rows
    quarter = 4 * rows
    d1 = wd.shape[1]
    half1 = d1 // 2

    def reduce_start(term, dest):
        def tile_of(which, ref):
            def body(j, _):
                start = pl.multiple_of(which * half1 + j * 256, 256)
                value = term(start)
                ref[:, :, pl.ds(pl.multiple_of(j * 256, 256), 256)] = value.reshape(4, quarter, 256)
                return 0

            lax.fori_loop(0, half1 // 256, body, 0)

        tile_of(1 - core, sib_out)
        swap = send(sib_out, sib_in, dc=1)
        tile_of(core, part)
        return swap

    def reduce_x(swap):
        arrive([swap])

        def body(i, _):
            total = part[i] + sib_in[i]
            part[i] = total
            xout[i] = total.astype(BF)
            return 0

        lax.fori_loop(0, 4, body, 0)
        return [send(xout.at[(x + d) % 4], xin.at[d - 1], dx=d) for d in near]

    def reduce_sum(moves, dest):
        arrive(moves)
        total = part[x]
        for d in range(3):
            total = total + xin[d].astype(F32)
        dest[core, x] = total.astype(BF)
        return [send(dest.at[core, x], dest.at[core, x], dx=d) for d in near]

    def reduce_relay(moves, dest):
        arrive(moves)
        return send(dest.at[core], dest.at[core], dc=1)

    loads[3].wait()

    def back_term(start):
        return dot_nt(cot[...].reshape(tokens, -1), wo[pl.ds(start, 256), :])

    swap = reduce_start(back_term, gm)
    moves = reduce_x(swap)
    loads[4].wait()
    spread = reduce_sum(moves, gm)
    relay = reduce_relay(spread, gm)
    arrive([relay])
    finish([swap, *moves])

    def block_rows(full, axis, d):
        out = []
        for h in range(2):
            if axis == "z":
                out.append(full[h, d])
            else:
                out.append(
                    jnp.concatenate([full[h, i, d * rows:(d + 1) * rows] for i in range(4)], axis=0)
                )
        return out

    def scatter_first(full, mult, o, inn, acc):
        copies = []
        for d in near:
            for s, axis in enumerate("zy"):
                left = block_rows(full, axis, d)
                o[s, d - 1] = mult(s, left).astype(BF)
                copies.append(send(o.at[s, d - 1], inn.at[s, d - 1], **{"d" + axis: d}))
        for s, axis in enumerate("zy"):
            acc[s] = mult(s, block_rows(full, axis, 0))
        return copies

    def scatter_second(copies, inn, acc, o2, in2):
        arrive(copies)
        out = []

        def summed(s, b):
            where = pl.ds(b * rows, rows)
            total = acc[s, where]
            for d in range(3):
                total = total + inn[s, d, where].astype(F32)
            return total

        for s, axis in enumerate("yz"):
            for d in near:
                o2[s, d - 1] = summed(s, d).astype(BF)
                out.append(send(o2.at[s, d - 1], in2.at[s, d - 1], **{"d" + axis: d}))
        for s in range(2):
            acc[s, 0:rows] = summed(s, 0)
        return out

    def scatter_last(copies, acc, in2, fin, ref, sem):
        arrive(copies)
        half = acc.shape[2]
        for s in range(2):
            total = acc[s, 0:rows]
            for d in range(3):
                total = total + in2[s, d].astype(F32)
            fin[:, s * half:(s + 1) * half] = total.astype(BF)
        copy = pltpu.make_async_copy(fin, ref, sem)
        copy.start()
        return copy

    ff = wd.shape[0]
    d2 = wo.shape[1]

    def hidden_mult(s, left):
        cols = slice(s * (ff // 2), (s + 1) * (ff // 2))
        return dot_nt(left[0], wd[cols, 0:half1]) + dot_nt(left[1], wd[cols, half1:])

    def out_mult(s, left):
        cols = slice(s * (d2 // 2), (s + 1) * (d2 // 2))
        return dot_nn(left[0], wo[0:half1, cols]) + dot_nn(left[1], wo[half1:, cols])

    g_first = scatter_first(gm, hidden_mult, g_out, g_in, g_acc)

    arrive(hid_second)

    def down_term(start):
        return dot_nn(hid[...].reshape(tokens, -1), wd[:, pl.ds(start, 256)])

    swap = reduce_start(down_term, dn)
    moves = reduce_x(swap)

    def weight_rows(left, right, ref, first, last):
        def out_copy(i, slot):
            return pltpu.make_async_copy(
                stage.at[slot, :, 0:ref.shape[1]], ref.at[pl.ds(pl.multiple_of(i * 256, 256), 256)], osem.at[slot]
            )

        def body(i, _):
            slot = i % 2

            @pl.when(i >= first + 2)
            def _():
                out_copy(i - 2, slot).wait()

            value = right(left(i).T)
            stage[slot, :, 0:ref.shape[1]] = value.astype(BF)
            out_copy(i, slot).start()
            return 0

        lax.fori_loop(first, last, body, 0)
        for i in (last - 2, last - 1):
            out_copy(i, i % 2).wait()

    def hid_cols(i):
        return hid[:, :, :, pl.ds(pl.multiple_of(i * 256, 256), 256)].reshape(tokens, 256)

    def times_gm(left):
        return jnp.concatenate(
            [dot_nn(left, gm[h].reshape(tokens, half1)) for h in range(2)], axis=1
        )

    blocks = ff // 256
    weight_rows(hid_cols, times_gm, gd_ref, 0, 4)
    spread = reduce_sum(moves, dn)
    weight_rows(hid_cols, times_gm, gd_ref, 4, 8)
    relay2 = reduce_relay(spread, dn)
    g_second = scatter_second(g_first, g_in, g_acc, g_out2, g_in2)
    arrive([relay2])
    p_first = scatter_first(dn, out_mult, p_out, p_in, p_acc)
    g_done = scatter_last(g_second, g_acc, g_in2, g_fin, gh_ref, lsem.at[5])

    per = half1 // 256

    def dn_cols(i):
        return dn[i // per, :, :, pl.ds(pl.multiple_of((i % per) * 256, 256), 256)].reshape(tokens, 256)

    def times_cot(left):
        return dot_nn(left, cot[...].reshape(tokens, d2))

    weight_rows(hid_cols, times_gm, gd_ref, 8, blocks)
    weight_rows(dn_cols, times_cot, go_ref, 0, 2)
    p_second = scatter_second(p_first, p_in, p_acc, p_out2, p_in2)
    weight_rows(dn_cols, times_cot, go_ref, 2, d1 // 256)
    p_done = scatter_last(p_second, p_acc, p_in2, p_fin, proj_ref, lsem.at[6])
    g_done.wait()
    p_done.wait()
    finish(list(sent))


def local(hidden_act, w_down, w_out, head_grad, token_ratio, pair_slot, segment_id):
    rows, ff = hidden_act.shape
    d1 = w_down.shape[1]
    d2 = w_out.shape[1]
    half1 = d1 // 2
    quarter = 4 * rows

    signed = (segment_id % 2).astype(F32) * (1 - 2 * (pair_slot % 2)).astype(F32)
    onehot = ((pair_slot // 2)[:, None] == jnp.arange(128, dtype=jnp.int32)[None, :]).astype(F32)
    tile = jnp.concatenate(
        [onehot * (signed * token_ratio)[:, None], onehot * signed[:, None]], axis=0
    )

    def reduce_shapes(width):
        half = width // 2
        return [
            pltpu.VMEM((2, 3, quarter, half), BF),
            pltpu.VMEM((2, 3, quarter, half), BF),
            pltpu.VMEM((2, quarter, half), F32),
            pltpu.VMEM((2, 3, rows, half), BF),
            pltpu.VMEM((2, 3, rows, half), BF),
            pltpu.VMEM((rows, width), BF),
        ]

    anywhere = pl.BlockSpec(memory_space=pl.ANY)
    copies = 80
    return pl.pallas_call(
        functools.partial(kernel, rows),
        out_shape=(
            jax.ShapeDtypeStruct((rows, d2), BF),
            jax.ShapeDtypeStruct((rows, ff), BF),
            jax.ShapeDtypeStruct((ff, d1), BF),
            jax.ShapeDtypeStruct((d1, d2), BF),
        ),
        in_specs=[anywhere] * 5,
        out_specs=[anywhere] * 4,
        scratch_shapes=[
            pltpu.VMEM((ff, d1), BF),
            pltpu.VMEM((d1, d2), BF),
            pltpu.VMEM((4, 4, rows, ff), BF),
            pltpu.VMEM((4, 4, rows, d2), BF),
            pltpu.VMEM((4, 4, rows, d2), BF),
            pltpu.VMEM((4, 4, 2 * rows, 128), F32),
            pltpu.VMEM((4, quarter, half1), F32),
            pltpu.VMEM((4, quarter, half1), F32),
            pltpu.VMEM((4, quarter, half1), F32),
            pltpu.VMEM((4, quarter, half1), BF),
            pltpu.VMEM((3, quarter, half1), BF),
            pltpu.VMEM((2, 4, quarter, half1), BF),
            pltpu.VMEM((2, 4, quarter, half1), BF),
            *reduce_shapes(ff),
            *reduce_shapes(d2),
            pltpu.VMEM((2, 256, d2), BF),
            pltpu.SemaphoreType.DMA((copies,)),
            pltpu.SemaphoreType.DMA((copies,)),
            pltpu.SemaphoreType.DMA((8,)),
            pltpu.SemaphoreType.DMA((2,)),
        ],
        compiler_params=pltpu.CompilerParams(
            collective_id=0, has_side_effects=True, vmem_limit_bytes=62 << 20
        ),
        cost_estimate=pl.CostEstimate(
            flops=6 * 16 * rows * d1 * (ff + d2),
            bytes_accessed=4 * d1 * (ff + d2),
            transcendentals=128,
        ),
    )(tile, hidden_act, w_down, w_out, head_grad)


def solution(mesh):
    placed = (
        P(("ia", "ka"), "ja"),
        P("ja", ("ia", "ka")),
        P(("ia", "ka"), "ja"),
        P(("ia", "ka"), "ja"),
        P(("ia", "ka")),
        P(("ia", "ka")),
        P(("ia", "ka")),
    )
    return jax.shard_map(
        local,
        mesh=mesh,
        in_specs=placed,
        out_specs=(
            P(("ia", "ka"), "ja"),
            P(("ia", "ka"), "ja"),
            P("ja", ("ia", "ka")),
            P(("ia", "ka"), "ja"),
        ),
        check_vma=False,
    )
```

time: 709 us -> 172 us (0.24)
  waiting for transfers between devices: 578 us -> 0 us
  Pallas kernels: 0 us -> 157 us
  matrix products: 55.8 us -> 0 us
  blocking collectives: 37.1 us -> 0 us
  between operations: 14.1 us -> 0.65 us
  other arithmetic: 10 us -> 2.07 us
    reduce_scatter x4 -> x0, waiting for transfers between devices: 386 us -> none  [the longest x2 318 us: scatter_rows(): lax.psum_scatter(term(jnp.int32(0), local_rows * lax.axis_size(('ia', 'ka...]
    all_gather x4 -> x0, waiting for transfers between devices: 191 us -> none  [the longest x2 147 us: gather_rows(): return lax.all_gather(block, ('ia', 'ka'), axis=0, tiled=True)]
    pallas_call x0 -> x1, Pallas kernels: none -> 157 us  [local(): pl.pallas_call(functools.partial(kernel, rows), out_shape=(jax.ShapeDtype...]
    dot_general x8 -> x0, matrix products: 55.8 us -> none  [the longest x2 19.4 us: contract_last(): lax.dot_general(left, right, (((1,), (1,)), ((), ())), preferred_element_...]
    psum x1 -> x0, blocking collectives: 37.1 us -> none  [local(): margin = lax.psum(local_margin, ('ia', 'ka'))]
    convert_element_type x5 -> x0, other arithmetic: 8.66 us -> none  [the longest x2 3.39 us: summed_middle(): shares = lax.psum_scatter(term(jnp.int32(0), total_rows // lax.axis_size(...]
  transfers between devices with their start and end apart: 8 -> 0, of which waited for: 8 -> 0; matrix products, arithmetic and copies ran while one was open for 10% -> 0% of each run, Pallas kernels for 0% -> 0%
where the time goes in v1:
time: 172 us; the launch traced here: 171 us
  Pallas kernels  157 us (91%)
  local copies, waits for them, and re-layouts  12.1 us (7%)
  other arithmetic  2.07 us (1%)
    pallas_call x1, Pallas kernels, local(): pl.pallas_call(functools.partial(kernel, rows), out_shape=(jax.ShapeDtype...  157 us
    unnamed x6, local copies, waits for them, and re-layouts  12.1 us

profile of v1, /device:TPU:1, one launch (start us, length us, event | category | flops | bytes accessed | tf_op | source)
XLA Modules:
  0.0 171.3 jit_solution(9470473308173578660)
XLA Ops:
  0.6 0.7 and_select_fusion.2
  1.3 0.7 fusion.8
  2.0 0.1 fusion.1
  2.1 0.6 pad_maximum_fusion.tile_ref
  2.7 156.5 %shard_map.102 = (bf16[48,2048]{1,0:T(8,128)(2,1)}, bf16[48,3328]{1,0:T(8,128)(2,1)}, bf16[3328,1024]{1,0:T(8,128)(2,1)}, bf16[1024,2048]{1,0:T(8,128)(2,1)}) custom-call(f32[96,128]{1,0:T(8,128)} %pad_maximum_fusion.tile_ref, bf16[48,3328]{1,0:T(8,128)(2,1)} %hid_ref.1, bf16[3328,1024]{1,0:T(8,128)(2,1)} %wd_ref.1, bf16[1024,2048]{1,0:T(8,128)(2,1)} %wo_ref.1, ...), custom_call_target="tpu_custom_call" | custom-call | flops 25367150592 | bytes 22020096 | tf_op jit(solution)/shard_map/pallas_call | solution.py:343
  159.2 1.6 copy.15
  160.8 1.7 copy.16
  162.6 0.0 copy-start
  162.6 6.8 %copy.17 = bf16[3328,1024]{1,0:T(8,128)(2,1)} copy(bf16[3328,1024]{1,0:T(8,128)(2,1)} %get-tuple-element.14) | data formatting | bytes 13631488
  169.3 0.0 copy-done
  169.3 2.0 %copy.18 = bf16[1024,2048]{1,0:T(8,128)(2,1)} copy(bf16[1024,2048]{1,0:T(8,128)(2,1)S(1)} %copy-done) | data formatting | bytes 8388608
Async XLA Ops:
  162.6 6.8 %copy-start = (bf16[1024,2048]{1,0:T(8,128)(2,1)S(1)}, bf16[1024,2048]{1,0:T(8,128)(2,1)}, u32[]{:S(2)}) copy-start(bf16[1024,2048]{1,0:T(8,128)(2,1)} %get-tuple-element.15) | copy-start | bytes 12582916

commit v2 on v1

--- a/solution.py
+++ b/solution.py
@@ -28,10 +28,9 @@
     proj_ref, gh_ref, gd_ref, go_ref,
     wd, wo, hid, hg, cot, tiles,
     sib_out, sib_in, part, xout, xin, gm, dn,
-    g_out, g_in, g_acc, g_out2, g_in2, g_fin,
-    p_out, p_in, p_acc, p_out2, p_in2, p_fin,
-    stage, ssem, rsem, lsem, osem,
+    *bufs,
 ):
+    g_bufs, p_bufs, (stage, ssem, rsem, lsem, osem) = bufs[:8], bufs[8:16], bufs[16:]
     ia, ja, ka = lax.axis_index("ia"), lax.axis_index("ja"), lax.axis_index("ka")
     z, y, x, core = ia * 2 + ka % 2, ka // 2, ja // 2, ja % 2
 
@@ -81,42 +80,100 @@
     for load in loads[:3]:
         load.wait()
 
-    def gather_first(full):
-        half = full.shape[3] // 2
-        lo, hi = pl.ds(0, half), pl.ds(half, half)
-        first = [
-            send(full.at[0, 0, :, lo], full.at[0, (4 - d) % 4, :, lo], dy=d) for d in near
-        ]
-        other = [
-            send(full.at[0, 0, :, hi], full.at[(4 - d) % 4, 0, :, hi], dz=d) for d in near
-        ]
-        return first, other
-
-    def gather_second(full, first, other):
-        half = full.shape[3] // 2
-        lo, hi = pl.ds(0, half), pl.ds(half, half)
-        arrive(first)
-        copies = [
-            send(full.at[0, :, :, lo], full.at[(4 - d) % 4, :, :, lo], dz=d) for d in near
-        ]
-        arrive(other)
-        return copies + [
-            send(full.at[:, 0, :, hi], full.at[:, (4 - d) % 4, :, hi], dy=d) for d in near
-        ]
-
+    class Gather:
+        def __init__(self, full):
+            self.full = full
+            self.width = full.shape[3] // 2
+            self.cut = self.width // 2 // 128 * 128
+            self.got = {}
+
+        def columns(self, s, part=None):
+            base = s * self.width
+            if part is None:
+                return pl.ds(base, self.width)
+            return pl.ds(base, self.cut) if part == 0 else pl.ds(base + self.cut, self.width - self.cut)
+
+        def slot(self, s, p, q, part=None):
+            cols = self.columns(s, part)
+            return self.full.at[q, p, :, cols] if s == 0 else self.full.at[p, q, :, cols]
+
+        def along(self, s, second, sign):
+            return {("dy", "dz")[(s + second) % 2]: sign}
+
+        def take(self, *key):
+            arrive([self.got.pop(key)])
+
+        def start_first(self):
+            for sign in (1, -1):
+                for s in (0, 1):
+                    self.got["p", s, sign] = send(
+                        self.slot(s, 0, 0), self.slot(s, -sign % 4, 0), **self.along(s, 0, sign)
+                    )
+
+        def across(self, s, p):
+            for sign in (1, -1):
+                self.got["s", s, p, sign] = send(
+                    self.slot(s, p, 0), self.slot(s, p, -sign % 4), **self.along(s, 1, sign)
+                )
+
+        def start_second(self):
+            for s in (0, 1):
+                self.across(s, 0)
+
+        def hand_on(self):
+            for sign in (1, -1):
+                for s in (0, 1):
+                    self.take("p", s, sign)
+                    part = 0 if sign == 1 else 1
+                    self.got["f", s, sign] = send(
+                        self.slot(s, -sign % 4, 0, part), self.slot(s, 2, 0, part), **self.along(s, 0, sign)
+                    )
+            for sign in (1, -1):
+                for s in (0, 1):
+                    self.across(s, -sign % 4)
+
+        def far(self):
+            for s in (0, 1):
+                self.take("f", s, 1)
+                self.take("f", s, -1)
+                self.across(s, 2)
+
+        def hand_across(self, p):
+            for sign in (1, -1):
+                for s in (0, 1):
+                    self.take("s", s, p, sign)
+                    self.take("s", s, p + 1, sign)
+                    part = 0 if sign == 1 else 1
+                    self.got["g", s, p, sign] = send(
+                        self.slot(s, pl.ds(p, 2), -sign % 4, part),
+                        self.slot(s, pl.ds(p, 2), 2, part),
+                        **self.along(s, 1, sign),
+                    )
+
+        def done(self):
+            for key in list(self.got):
+                self.take(*key)
+
+    grad_rows, hidden_rows = Gather(hg), Gather(hid)
     tile_first = [send(tiles.at[0, 0], tiles.at[0, (4 - d) % 4], dy=d) for d in near]
-    hg_first = gather_first(hg)
-    hid_first = gather_first(hid)
+    grad_rows.start_first()
+    grad_rows.start_second()
+    hidden_rows.start_first()
     arrive(tile_first)
     tile_second = [send(tiles.at[0], tiles.at[(4 - d) % 4], dz=d) for d in near]
-    hg_second = gather_second(hg, *hg_first)
-    hid_second = gather_second(hid, *hid_first)
+    grad_rows.hand_on()
+    grad_rows.far()
+    hidden_rows.start_second()
+    grad_rows.hand_across(0)
+    grad_rows.hand_across(2)
+    hidden_rows.hand_on()
+    hidden_rows.far()
 
     arrive(tile_second)
     margin = jnp.sum(tiles[:, :, 0:rows, :], axis=(0, 1, 2))[None, :]
     weight = -beta_scale * jax.nn.sigmoid(-beta_scale * margin)
 
-    arrive(hg_second)
+    grad_rows.done()
 
     def scale(i, _):
         coef = jnp.sum(tiles[i // 4, i % 4, rows:, :] * weight, axis=1, keepdims=True)
@@ -130,20 +187,13 @@
     d1 = wd.shape[1]
     half1 = d1 // 2
 
-    def reduce_start(term, dest):
-        def tile_of(which, ref):
-            def body(j, _):
-                start = pl.multiple_of(which * half1 + j * 256, 256)
-                value = term(start)
-                ref[:, :, pl.ds(pl.multiple_of(j * 256, 256), 256)] = value.reshape(4, quarter, 256)
-                return 0
-
-            lax.fori_loop(0, half1 // 256, body, 0)
-
-        tile_of(1 - core, sib_out)
-        swap = send(sib_out, sib_in, dc=1)
-        tile_of(core, part)
-        return swap
+    def partial_sum(term, which, ref):
+        def body(j, _):
+            value = term(pl.multiple_of(which * half1 + j * 256, 256))
+            ref[:, :, pl.ds(pl.multiple_of(j * 256, 256), 256)] = value.reshape(4, quarter, 256)
+            return 0
+
+        lax.fori_loop(0, half1 // 256, body, 0)
 
     def reduce_x(swap):
         arrive([swap])
@@ -174,13 +224,24 @@
     def back_term(start):
         return dot_nt(cot[...].reshape(tokens, -1), wo[pl.ds(start, 256), :])
 
-    swap = reduce_start(back_term, gm)
+    partial_sum(back_term, 1 - core, sib_out)
+    swap = send(sib_out, sib_in, dc=1)
+    hidden_rows.hand_across(0)
+    partial_sum(back_term, core, part)
+    hidden_rows.hand_across(2)
     moves = reduce_x(swap)
     loads[4].wait()
     spread = reduce_sum(moves, gm)
+    finish([swap, *moves])
+    hidden_rows.done()
+
+    def down_term(start):
+        return dot_nn(hid[...].reshape(tokens, -1), wd[:, pl.ds(start, 256)])
+
+    partial_sum(down_term, 1 - core, sib_out)
     relay = reduce_relay(spread, gm)
     arrive([relay])
-    finish([swap, *moves])
+    swap = send(sib_out, sib_in, dc=1)
 
     def block_rows(full, axis, d):
         out = []
@@ -193,68 +254,91 @@
                 )
         return out
 
-    def scatter_first(full, mult, o, inn, acc):
-        copies = []
-        for d in near:
-            for s, axis in enumerate("zy"):
-                left = block_rows(full, axis, d)
-                o[s, d - 1] = mult(s, left).astype(BF)
-                copies.append(send(o.at[s, d - 1], inn.at[s, d - 1], **{"d" + axis: d}))
-        for s, axis in enumerate("zy"):
-            acc[s] = mult(s, block_rows(full, axis, 0))
-        return copies
-
-    def scatter_second(copies, inn, acc, o2, in2):
-        arrive(copies)
-        out = []
-
-        def summed(s, b):
-            where = pl.ds(b * rows, rows)
-            total = acc[s, where]
-            for d in range(3):
-                total = total + inn[s, d, where].astype(F32)
-            return total
-
-        for s, axis in enumerate("yz"):
-            for d in near:
-                o2[s, d - 1] = summed(s, d).astype(BF)
-                out.append(send(o2.at[s, d - 1], in2.at[s, d - 1], **{"d" + axis: d}))
-        for s in range(2):
-            acc[s, 0:rows] = summed(s, 0)
-        return out
-
-    def scatter_last(copies, acc, in2, fin, ref, sem):
-        arrive(copies)
-        half = acc.shape[2]
-        for s in range(2):
-            total = acc[s, 0:rows]
-            for d in range(3):
-                total = total + in2[s, d].astype(F32)
-            fin[:, s * half:(s + 1) * half] = total.astype(BF)
-        copy = pltpu.make_async_copy(fin, ref, sem)
-        copy.start()
-        return copy
+    class Scatter:
+        def __init__(self, full, mult, acc, out, relay, inn, out2, relay2, inn2, fin):
+            self.full, self.mult, self.acc, self.fin = full, mult, acc, fin
+            self.stages = ((out, relay, inn), (out2, relay2, inn2))
+            self.width = acc.shape[2]
+            cut = self.width // 2 // 128 * 128
+            self.parts = (slice(0, cut), slice(cut, self.width))
+            self.got = {}
+
+        def axis(self, s, stage):
+            return "zy"[(s + stage) % 2]
+
+        def term(self, s, stage, d, part):
+            if stage == 0:
+                return self.mult(s, block_rows(self.full, self.axis(s, 0), d), part)
+            return self.acc[s, d * rows:(d + 1) * rows, part]
+
+        def move(self, key, s, stage, d, part, value, dst, sign):
+            out = self.stages[stage][0]
+            cols = pl.ds(part.start, part.stop - part.start)
+            out[s, d - 1, :, part] = value.astype(BF)
+            self.got[key, s, stage, sign] = send(
+                out.at[s, d - 1, :, cols], dst.at[:, cols], **{"d" + self.axis(s, stage): sign}
+            )
+
+        def take(self, key, s, stage, sign):
+            arrive([self.got.pop((key, s, stage, sign))])
+
+        def far(self, s, stage):
+            relay = self.stages[stage][1]
+            for part, sign in zip(self.parts, (1, -1)):
+                self.move("relay", s, stage, 2, part, self.term(s, stage, 2, part), relay.at[s], sign)
+
+        def direct(self, s, stage):
+            inn = self.stages[stage][2]
+            for part, sign in zip(self.parts[::-1], (1, -1)):
+                d = sign % 4
+                self.move("direct", s, stage, d, part, self.term(s, stage, d, part), inn.at[s, d // 2], sign)
+
+        def joined(self, s, stage):
+            relay, inn = self.stages[stage][1:]
+            for part, sign in zip(self.parts, (1, -1)):
+                d = sign % 4
+                value = self.term(s, stage, d, part)
+                self.take("relay", s, stage, sign)
+                value = value + relay[s, :, part].astype(F32)
+                self.move("joined", s, stage, d, part, value, inn.at[s, d // 2], sign)
+
+        def own(self, s):
+            for part in self.parts:
+                self.acc[s, :, part] = self.term(s, 0, 0, part)
+
+        def total(self, s):
+            inn = self.stages[0][2]
+            for key in ("direct", "joined"):
+                for sign in (1, -1):
+                    self.take(key, s, 0, sign)
+            self.acc[s] = self.acc[s] + inn[s, 0].astype(F32) + inn[s, 1].astype(F32)
+
+        def last(self, ref, sem):
+            inn = self.stages[1][2]
+            for s in (0, 1):
+                for key in ("direct", "joined"):
+                    for sign in (1, -1):
+                        self.take(key, s, 1, sign)
+                value = self.acc[s, 0:rows] + inn[s, 0].astype(F32) + inn[s, 1].astype(F32)
+                self.fin[:, s * self.width:(s + 1) * self.width] = value.astype(BF)
+            copy = pltpu.make_async_copy(self.fin, ref, sem)
+            copy.start()
+            return copy
 
     ff = wd.shape[0]
     d2 = wo.shape[1]
 
-    def hidden_mult(s, left):
-        cols = slice(s * (ff // 2), (s + 1) * (ff // 2))
+    def hidden_mult(s, left, part):
+        cols = slice(s * (ff // 2) + part.start, s * (ff // 2) + part.stop)
         return dot_nt(left[0], wd[cols, 0:half1]) + dot_nt(left[1], wd[cols, half1:])
 
-    def out_mult(s, left):
-        cols = slice(s * (d2 // 2), (s + 1) * (d2 // 2))
+    def out_mult(s, left, part):
+        cols = slice(s * (d2 // 2) + part.start, s * (d2 // 2) + part.stop)
         return dot_nn(left[0], wo[0:half1, cols]) + dot_nn(left[1], wo[half1:, cols])
 
-    g_first = scatter_first(gm, hidden_mult, g_out, g_in, g_acc)
-
-    arrive(hid_second)
-
-    def down_term(start):
-        return dot_nn(hid[...].reshape(tokens, -1), wd[:, pl.ds(start, 256)])
-
-    swap = reduce_start(down_term, dn)
-    moves = reduce_x(swap)
+    grad_hidden = Scatter(gm, hidden_mult, *g_bufs)
+    projected = Scatter(dn, out_mult, *p_bufs)
+    hid_blocks = ff // 256
 
     def weight_rows(left, right, ref, first, last):
         def out_copy(i, slot):
@@ -286,16 +370,6 @@
             [dot_nn(left, gm[h].reshape(tokens, half1)) for h in range(2)], axis=1
         )
 
-    blocks = ff // 256
-    weight_rows(hid_cols, times_gm, gd_ref, 0, 4)
-    spread = reduce_sum(moves, dn)
-    weight_rows(hid_cols, times_gm, gd_ref, 4, 8)
-    relay2 = reduce_relay(spread, dn)
-    g_second = scatter_second(g_first, g_in, g_acc, g_out2, g_in2)
-    arrive([relay2])
-    p_first = scatter_first(dn, out_mult, p_out, p_in, p_acc)
-    g_done = scatter_last(g_second, g_acc, g_in2, g_fin, gh_ref, lsem.at[5])
-
     per = half1 // 256
 
     def dn_cols(i):
@@ -304,11 +378,55 @@
     def times_cot(left):
         return dot_nn(left, cot[...].reshape(tokens, d2))
 
-    weight_rows(hid_cols, times_gm, gd_ref, 8, blocks)
-    weight_rows(dn_cols, times_cot, go_ref, 0, 2)
-    p_second = scatter_second(p_first, p_in, p_acc, p_out2, p_in2)
-    weight_rows(dn_cols, times_cot, go_ref, 2, d1 // 256)
-    p_done = scatter_last(p_second, p_acc, p_in2, p_fin, proj_ref, lsem.at[6])
+    def down_rows(first, last):
+        weight_rows(hid_cols, times_gm, gd_ref, first, last)
+
+    def out_rows(first, last):
+        weight_rows(dn_cols, times_cot, go_ref, first, last)
+
+    for s in (0, 1):
+        grad_hidden.far(s, 0)
+    partial_sum(down_term, core, part)
+    moves = reduce_x(swap)
+    for s in (0, 1):
+        grad_hidden.direct(s, 0)
+    for s in (0, 1):
+        grad_hidden.joined(s, 0)
+    for s in (0, 1):
+        grad_hidden.own(s)
+    down_rows(0, 2)
+    spread = reduce_sum(moves, dn)
+    down_rows(2, 8)
+    for s in (0, 1):
+        grad_hidden.total(s)
+        grad_hidden.far(s, 1)
+    for s in (0, 1):
+        grad_hidden.direct(s, 1)
+    relay2 = reduce_relay(spread, dn)
+    for s in (0, 1):
+        grad_hidden.joined(s, 1)
+    arrive([relay2])
+    for s in (0, 1):
+        projected.far(s, 0)
+    for s in (0, 1):
+        projected.direct(s, 0)
+    g_done = grad_hidden.last(gh_ref, lsem.at[5])
+    down_rows(8, 10)
+    for s in (0, 1):
+        projected.joined(s, 0)
+    for s in (0, 1):
+        projected.own(s)
+    down_rows(10, hid_blocks)
+    for s in (0, 1):
+        projected.total(s)
+        projected.far(s, 1)
+    for s in (0, 1):
+        projected.direct(s, 1)
+    out_rows(0, 2)
+    for s in (0, 1):
+        projected.joined(s, 1)
+    out_rows(2, d1 // 256)
+    p_done = projected.last(proj_ref, lsem.at[6])
     g_done.wait()
     p_done.wait()
     finish(list(sent))
@@ -329,17 +447,17 @@
 
     def reduce_shapes(width):
         half = width // 2
-        return [
-            pltpu.VMEM((2, 3, quarter, half), BF),
-            pltpu.VMEM((2, 3, quarter, half), BF),
-            pltpu.VMEM((2, quarter, half), F32),
-            pltpu.VMEM((2, 3, rows, half), BF),
-            pltpu.VMEM((2, 3, rows, half), BF),
-            pltpu.VMEM((rows, width), BF),
-        ]
+        shapes = [pltpu.VMEM((2, quarter, half), F32)]
+        for count in (quarter, rows):
+            shapes += [
+                pltpu.VMEM((2, 3, count, half), BF),
+                pltpu.VMEM((2, count, half), BF),
+                pltpu.VMEM((2, 2, count, half), BF),
+            ]
+        return shapes + [pltpu.VMEM((rows, width), BF)]
 
     anywhere = pl.BlockSpec(memory_space=pl.ANY)
-    copies = 80
+    copies = 144
     return pl.pallas_call(
         functools.partial(kernel, rows),
         out_shape=(

time: 172 us -> 148 us (0.86)
  Pallas kernels: 157 us -> 133 us
    pallas_call x1, Pallas kernels: 157 us -> 133 us  [local(): pl.pallas_call(functools.partial(kernel, rows), out_shape=(jax.ShapeDtype...]
where the time goes in v2:
time: 148 us; the launch traced here: 147 us
  Pallas kernels  133 us (90%)
  local copies, waits for them, and re-layouts  12.1 us (8%)
  other arithmetic  2.07 us (1%)
    pallas_call x1, Pallas kernels, local(): pl.pallas_call(functools.partial(kernel, rows), out_shape=(jax.ShapeDtype...  133 us
    unnamed x6, local copies, waits for them, and re-layouts  12.1 us

profile of v2, /device:TPU:1, one launch (start us, length us, event | category | flops | bytes accessed | tf_op | source)
XLA Modules:
  0.0 147.4 jit_solution(5671296136636163685)
XLA Ops:
  0.6 0.7 and_select_fusion.2
  1.3 0.7 fusion.8
  2.0 0.1 fusion.1
  2.1 0.6 pad_maximum_fusion.tile_ref
  2.7 132.6 %shard_map.102 = (bf16[48,2048]{1,0:T(8,128)(2,1)}, bf16[48,3328]{1,0:T(8,128)(2,1)}, bf16[3328,1024]{1,0:T(8,128)(2,1)}, bf16[1024,2048]{1,0:T(8,128)(2,1)}) custom-call(f32[96,128]{1,0:T(8,128)} %pad_maximum_fusion.tile_ref, bf16[48,3328]{1,0:T(8,128)(2,1)} %hid_ref.1, bf16[3328,1024]{1,0:T(8,128)(2,1)} %wd_ref.1, bf16[1024,2048]{1,0:T(8,128)(2,1)} %wo_ref.1, ...), custom_call_target="tpu_custom_call" | custom-call | flops 25367150592 | bytes 22020096 | tf_op jit(solution)/shard_map/pallas_call | solution.py:461
  135.3 1.6 %copy.15 = bf16[48,2048]{1,0:T(8,128)(2,1)} copy(bf16[48,2048]{1,0:T(8,128)(2,1)} %get-tuple-element.12) | data formatting | bytes 393216
  136.9 1.7 %copy.16 = bf16[48,3328]{1,0:T(8,128)(2,1)} copy(bf16[48,3328]{1,0:T(8,128)(2,1)} %get-tuple-element.13) | data formatting | bytes 638976
  138.6 0.0 copy-start
  138.6 6.8 %copy.17 = bf16[3328,1024]{1,0:T(8,128)(2,1)} copy(bf16[3328,1024]{1,0:T(8,128)(2,1)} %get-tuple-element.14) | data formatting | bytes 13631488
  145.4 0.0 copy-done
  145.4 2.0 %copy.18 = bf16[1024,2048]{1,0:T(8,128)(2,1)} copy(bf16[1024,2048]{1,0:T(8,128)(2,1)S(1)} %copy-done) | data formatting | bytes 8388608
Async XLA Ops:
  138.6 6.8 %copy-start = (bf16[1024,2048]{1,0:T(8,128)(2,1)S(1)}, bf16[1024,2048]{1,0:T(8,128)(2,1)}, u32[]{:S(2)}) copy-start(bf16[1024,2048]{1,0:T(8,128)(2,1)} %get-tuple-element.15) | copy-start | bytes 12582916

commit v3 on v2

--- a/solution.py
+++ b/solution.py
@@ -7,7 +7,6 @@
 from jax.experimental.pallas import tpu as pltpu
 from jax.sharding import PartitionSpec as P
 
-PAIRS = 8
 MESH = pl.DeviceIdType.MESH
 BF = jnp.bfloat16
 F32 = jnp.float32
@@ -24,7 +23,7 @@
 
 
 def kernel(
-    rows, tile_ref, hid_ref, wd_ref, wo_ref, hg_ref,
+    rows, ratio_ref, slot_ref, segment_ref, hid_ref, wd_ref, wo_ref, hg_ref,
     proj_ref, gh_ref, gd_ref, go_ref,
     wd, wo, hid, hg, cot, tiles,
     sib_out, sib_in, part, xout, xin, gm, dn,
@@ -65,19 +64,24 @@
     loads = [
         pltpu.make_async_copy(hg_ref, hg.at[0, 0], lsem.at[0]),
         pltpu.make_async_copy(hid_ref, hid.at[0, 0], lsem.at[1]),
-        pltpu.make_async_copy(tile_ref, tiles.at[0, 0], lsem.at[2]),
-        pltpu.make_async_copy(wo_ref, wo, lsem.at[3]),
-        pltpu.make_async_copy(wd_ref, wd, lsem.at[4]),
+        pltpu.make_async_copy(wo_ref, wo, lsem.at[2]),
+        pltpu.make_async_copy(wd_ref, wd, lsem.at[3]),
     ]
     for load in loads:
         load.start()
+
+    sign = ((segment_ref[...] & 1) * (1 - 2 * (slot_ref[...] & 1))).astype(F32)
+    tiles[0, 0] = jnp.full((8, 128), -1.0, F32)
+    tiles[0, 0, 0:1, 0:rows] = sign * ratio_ref[...]
+    tiles[0, 0, 1:2, 0:rows] = (slot_ref[...] >> 1).astype(F32)
+    tiles[0, 0, 2:3, 0:rows] = sign
 
     barrier = pltpu.get_barrier_semaphore()
     peers = [dict(dc=1)] + [{a: d} for a in ("dx", "dy", "dz") for d in near]
     for where in peers:
         pl.semaphore_signal(barrier, inc=1, device_id=peer(**where), device_id_type=MESH)
     pl.semaphore_wait(barrier, len(peers))
-    for load in loads[:3]:
+    for load in loads[:2]:
         load.wait()
 
     class Gather:
@@ -155,8 +159,8 @@
                 self.take(*key)
 
     grad_rows, hidden_rows = Gather(hg), Gather(hid)
+    grad_rows.start_first()
     tile_first = [send(tiles.at[0, 0], tiles.at[0, (4 - d) % 4], dy=d) for d in near]
-    grad_rows.start_first()
     grad_rows.start_second()
     hidden_rows.start_first()
     arrive(tile_first)
@@ -166,82 +170,115 @@
     hidden_rows.start_second()
     grad_rows.hand_across(0)
     grad_rows.hand_across(2)
-    hidden_rows.hand_on()
-    hidden_rows.far()
 
     arrive(tile_second)
-    margin = jnp.sum(tiles[:, :, 0:rows, :], axis=(0, 1, 2))[None, :]
+    pairs = lax.broadcasted_iota(jnp.int32, (8, 128), 0).astype(F32)
+
+    def add_margin(i, total):
+        tile = tiles[i // 4, i % 4]
+        return total + jnp.where(tile[1:2] == pairs, tile[0:1], 0.0)
+
+    margin = jnp.sum(
+        lax.fori_loop(0, 16, add_margin, jnp.zeros((8, 128), F32)), axis=1, keepdims=True
+    )
     weight = -beta_scale * jax.nn.sigmoid(-beta_scale * margin)
 
-    grad_rows.done()
-
     def scale(i, _):
-        coef = jnp.sum(tiles[i // 4, i % 4, rows:, :] * weight, axis=1, keepdims=True)
+        tile = tiles[i // 4, i % 4]
+        line = jnp.sum(jnp.where(tile[1:2] == pairs, weight, 0.0), axis=0, keepdims=True) * tile[2:3]
+        coef = jnp.broadcast_to(line, (8, 128)).T[0:rows, 0:1]
         cot[i // 4, i % 4] = (coef * hg[i // 4, i % 4].astype(F32)).astype(BF)
         return 0
-
-    lax.fori_loop(0, 16, scale, 0)
 
     tokens = 16 * rows
     quarter = 4 * rows
     d1 = wd.shape[1]
     half1 = d1 // 2
 
-    def partial_sum(term, which, ref):
-        def body(j, _):
-            value = term(pl.multiple_of(which * half1 + j * 256, 256))
-            ref[:, :, pl.ds(pl.multiple_of(j * 256, 256), 256)] = value.reshape(4, quarter, 256)
-            return 0
-
-        lax.fori_loop(0, half1 // 256, body, 0)
-
-    def reduce_x(swap):
-        arrive([swap])
-
-        def body(i, _):
-            total = part[i] + sib_in[i]
-            part[i] = total
-            xout[i] = total.astype(BF)
-            return 0
-
-        lax.fori_loop(0, 4, body, 0)
-        return [send(xout.at[(x + d) % 4], xin.at[d - 1], dx=d) for d in near]
-
-    def reduce_sum(moves, dest):
-        arrive(moves)
-        total = part[x]
-        for d in range(3):
-            total = total + xin[d].astype(F32)
-        dest[core, x] = total.astype(BF)
-        return [send(dest.at[core, x], dest.at[core, x], dx=d) for d in near]
-
-    def reduce_relay(moves, dest):
-        arrive(moves)
-        return send(dest.at[core], dest.at[core], dc=1)
-
-    loads[3].wait()
+    class Reduce:
+        def __init__(self, term, dest):
+            self.term, self.dest = term, dest
+            self.swaps, self.moves, self.spread, self.relays = {}, {}, {}, {}
+
+        def fill(self, j, which, ref):
+            value = self.term(pl.multiple_of(which * half1 + j * 256, 256))
+            ref[j] = value.reshape(4, quarter, 256)
+
+        def theirs(self, j):
+            self.fill(j, 1 - core, sib_out)
+
+        def swap(self, j):
+            self.swaps[j] = send(sib_out.at[j], sib_in.at[j], dc=1)
+
+        def mine(self, j):
+            self.fill(j, core, part)
+
+        def start(self, j):
+            arrive([self.swaps[j]])
+
+            def body(i, _):
+                total = part[j, i] + sib_in[j, i]
+                part[j, i] = total
+                xout[j, i] = total.astype(BF)
+                return 0
+
+            lax.fori_loop(0, 4, body, 0)
+            self.moves[j] = [send(xout.at[j, (x + d) % 4], xin.at[j, d - 1], dx=d) for d in near]
+
+        def sum(self, j):
+            arrive(self.moves[j])
+            finish([self.swaps[j]])
+            total = part[j, x]
+            for d in range(3):
+                total = total + xin[j, d].astype(F32)
+            cols = slice(j * 256, j * 256 + 256)
+            self.dest[core, x, :, cols] = total.astype(BF)
+            spot = self.dest.at[core, x, :, pl.ds(j * 256, 256)]
+            self.spread[j] = [send(spot, spot, dx=d) for d in near]
+
+        def relay(self, j):
+            arrive(self.spread[j])
+            spot = self.dest.at[core, :, :, pl.ds(j * 256, 256)]
+            self.relays[j] = send(spot, spot, dc=1)
+
+        def done(self, j):
+            arrive([self.relays[j]])
+            finish(self.moves[j])
 
     def back_term(start):
         return dot_nt(cot[...].reshape(tokens, -1), wo[pl.ds(start, 256), :])
 
-    partial_sum(back_term, 1 - core, sib_out)
-    swap = send(sib_out, sib_in, dc=1)
-    hidden_rows.hand_across(0)
-    partial_sum(back_term, core, part)
-    hidden_rows.hand_across(2)
-    moves = reduce_x(swap)
-    loads[4].wait()
-    spread = reduce_sum(moves, gm)
-    finish([swap, *moves])
-    hidden_rows.done()
-
     def down_term(start):
         return dot_nn(hid[...].reshape(tokens, -1), wd[:, pl.ds(start, 256)])
 
-    partial_sum(down_term, 1 - core, sib_out)
-    relay = reduce_relay(spread, gm)
-    arrive([relay])
-    swap = send(sib_out, sib_in, dc=1)
+    sum_back, sum_down = Reduce(back_term, gm), Reduce(down_term, dn)
+
+    grad_rows.done()
+    hidden_rows.hand_on()
+    lax.fori_loop(0, 16, scale, 0)
+    loads[2].wait()
+    sum_back.theirs(0)
+    sum_back.swap(0)
+    hidden_rows.far()
+    sum_back.mine(0)
+    sum_back.start(0)
+    sum_back.theirs(1)
+    sum_back.swap(1)
+    hidden_rows.hand_across(0)
+    sum_back.mine(1)
+    sum_back.start(1)
+    hidden_rows.hand_across(2)
+    sum_back.sum(0)
+    loads[3].wait()
+    sum_back.sum(1)
+    sum_back.relay(0)
+    hidden_rows.done()
+    sum_down.theirs(0)
+    sum_back.done(0)
+    sum_down.swap(0)
+    sum_back.relay(1)
+    sum_down.mine(0)
+    sum_back.done(1)
 
     def block_rows(full, axis, d):
         out = []
@@ -384,52 +421,75 @@
     def out_rows(first, last):
         weight_rows(dn_cols, times_cot, go_ref, first, last)
 
+    sum_down.start(0)
     for s in (0, 1):
         grad_hidden.far(s, 0)
-    partial_sum(down_term, core, part)
-    moves = reduce_x(swap)
+    sum_down.theirs(1)
+    sum_down.swap(1)
+    sum_down.mine(1)
+    sum_down.start(1)
     for s in (0, 1):
         grad_hidden.direct(s, 0)
+    sum_down.sum(0)
     for s in (0, 1):
         grad_hidden.joined(s, 0)
+    sum_down.sum(1)
     for s in (0, 1):
         grad_hidden.own(s)
     down_rows(0, 2)
-    spread = reduce_sum(moves, dn)
-    down_rows(2, 8)
+    sum_down.relay(0)
+    down_rows(2, 4)
+    sum_down.relay(1)
+    sum_down.done(0)
+    sum_down.done(1)
+    for s in (0, 1):
+        projected.far(s, 0)
+    for s in (0, 1):
+        projected.direct(s, 0)
+    down_rows(4, 6)
     for s in (0, 1):
         grad_hidden.total(s)
         grad_hidden.far(s, 1)
     for s in (0, 1):
         grad_hidden.direct(s, 1)
-    relay2 = reduce_relay(spread, dn)
+    for s in (0, 1):
+        projected.joined(s, 0)
     for s in (0, 1):
         grad_hidden.joined(s, 1)
-    arrive([relay2])
-    for s in (0, 1):
-        projected.far(s, 0)
-    for s in (0, 1):
-        projected.direct(s, 0)
-    g_done = grad_hidden.last(gh_ref, lsem.at[5])
-    down_rows(8, 10)
-    for s in (0, 1):
-        projected.joined(s, 0)
     for s in (0, 1):
         projected.own(s)
-    down_rows(10, hid_blocks)
+    down_rows(6, hid_blocks)
+    g_done = grad_hidden.last(gh_ref, lsem.at[4])
+    out_rows(0, 2)
     for s in (0, 1):
         projected.total(s)
         projected.far(s, 1)
     for s in (0, 1):
         projected.direct(s, 1)
-    out_rows(0, 2)
     for s in (0, 1):
         projected.joined(s, 1)
     out_rows(2, d1 // 256)
-    p_done = projected.last(proj_ref, lsem.at[6])
+    p_done = projected.last(proj_ref, lsem.at[5])
     g_done.wait()
     p_done.wait()
     finish(list(sent))
+
+
+def keep(*refs):
+    loads, stores = [], []
+    for source, target, held, pieces in zip(refs[:4], refs[4:8], refs[8:12], (1, 1, 13, 8)):
+        count = source.shape[0] // pieces
+        for i in range(pieces):
+            where, n = pl.ds(i * count, count), len(loads)
+            loads.append(pltpu.make_async_copy(source.at[where], held.at[where], refs[12].at[n]))
+            stores.append(pltpu.make_async_copy(held.at[where], target.at[where], refs[13].at[n]))
+    for load in loads:
+        load.start()
+    for load, store in zip(loads, stores):
+        load.wait()
+        store.start()
+    for store in stores:
+        store.wait()
 
 
 def local(hidden_act, w_down, w_out, head_grad, token_ratio, pair_slot, segment_id):
@@ -438,12 +498,6 @@
     d2 = w_out.shape[1]
     half1 = d1 // 2
     quarter = 4 * rows
-
-    signed = (segment_id % 2).astype(F32) * (1 - 2 * (pair_slot % 2)).astype(F32)
-    onehot = ((pair_slot // 2)[:, None] == jnp.arange(128, dtype=jnp.int32)[None, :]).astype(F32)
-    tile = jnp.concatenate(
-        [onehot * (signed * token_ratio)[:, None], onehot * signed[:, None]], axis=0
-    )
 
     def reduce_shapes(width):
         half = width // 2
@@ -457,8 +511,8 @@
         return shapes + [pltpu.VMEM((rows, width), BF)]
 
     anywhere = pl.BlockSpec(memory_space=pl.ANY)
-    copies = 144
-    return pl.pallas_call(
+    copies = 160
+    results = pl.pallas_call(
         functools.partial(kernel, rows),
         out_shape=(
             jax.ShapeDtypeStruct((rows, d2), BF),
@@ -466,7 +520,7 @@
             jax.ShapeDtypeStruct((ff, d1), BF),
             jax.ShapeDtypeStruct((d1, d2), BF),
         ),
-        in_specs=[anywhere] * 5,
+        in_specs=[pl.BlockSpec(memory_space=pltpu.VMEM)] * 3 + [anywhere] * 4,
         out_specs=[anywhere] * 4,
         scratch_shapes=[
             pltpu.VMEM((ff, d1), BF),
@@ -474,12 +528,12 @@
             pltpu.VMEM((4, 4, rows, ff), BF),
             pltpu.VMEM((4, 4, rows, d2), BF),
             pltpu.VMEM((4, 4, rows, d2), BF),
-            pltpu.VMEM((4, 4, 2 * rows, 128), F32),
-            pltpu.VMEM((4, quarter, half1), F32),
-            pltpu.VMEM((4, quarter, half1), F32),
-            pltpu.VMEM((4, quarter, half1), F32),
-            pltpu.VMEM((4, quarter, half1), BF),
-            pltpu.VMEM((3, quarter, half1), BF),
+            pltpu.VMEM((4, 4, 8, 128), F32),
+            pltpu.VMEM((2, 4, quarter, 256), F32),
+            pltpu.VMEM((2, 4, quarter, 256), F32),
+            pltpu.VMEM((2, 4, quarter, 256), F32),
+            pltpu.VMEM((2, 4, quarter, 256), BF),
+            pltpu.VMEM((2, 3, quarter, 256), BF),
             pltpu.VMEM((2, 4, quarter, half1), BF),
             pltpu.VMEM((2, 4, quarter, half1), BF),
             *reduce_shapes(ff),
@@ -487,7 +541,7 @@
             pltpu.VMEM((2, 256, d2), BF),
             pltpu.SemaphoreType.DMA((copies,)),
             pltpu.SemaphoreType.DMA((copies,)),
-            pltpu.SemaphoreType.DMA((8,)),
+            pltpu.SemaphoreType.DMA((6,)),
             pltpu.SemaphoreType.DMA((2,)),
         ],
         compiler_params=pltpu.CompilerParams(
@@ -498,7 +552,21 @@
             bytes_accessed=4 * d1 * (ff + d2),
             transcendentals=128,
         ),
-    )(tile, hidden_act, w_down, w_out, head_grad)
+    )(
+        token_ratio[None], pair_slot[None], segment_id[None], hidden_act, w_down, w_out, head_grad
+    )
+    return pl.pallas_call(
+        keep,
+        out_shape=[jax.ShapeDtypeStruct(r.shape, r.dtype) for r in results],
+        in_specs=[anywhere] * 4,
+        out_specs=[anywhere] * 4,
+        scratch_shapes=[pltpu.VMEM(r.shape, r.dtype) for r in results]
+        + [pltpu.SemaphoreType.DMA((24,)), pltpu.SemaphoreType.DMA((24,))],
+        compiler_params=pltpu.CompilerParams(vmem_limit_bytes=32 << 20),
+        cost_estimate=pl.CostEstimate(
+            flops=0, bytes_accessed=4 * d1 * (ff + d2), transcendentals=0
+        ),
+    )(*results)
 
 
 def solution(mesh):

time: 148 us -> 139 us (0.939)
  local copies, waits for them, and re-layouts: 12.1 us -> 7.01 us
  other arithmetic: 2.07 us -> 0 us
  Pallas kernels: 133 us -> 131 us
    pallas_call x1, Pallas kernels: 133 us -> 125 us  [local(): pl.pallas_call(functools.partial(kernel, rows), out_shape=(jax.ShapeDtype...]
    pallas_call x0 -> x1, Pallas kernels: none -> 5.72 us  [local(): pl.pallas_call(keep, out_shape=[jax.ShapeDtypeStruct(r.shape, r.dtype) fo...]
    unnamed x6 -> x8, local copies, waits for them, and re-layouts: 12.1 us -> 7.01 us
where the time goes in v3:
time: 139 us
  Pallas kernels  131 us (94%)
  local copies, waits for them, and re-layouts  7.01 us (5%)
    pallas_call x1, Pallas kernels, local(): pl.pallas_call(functools.partial(kernel, rows), out_shape=(jax.ShapeDtype...  125 us
    unnamed x8, local copies, waits for them, and re-layouts  7.01 us
    pallas_call x1, Pallas kernels, local(): pl.pallas_call(keep, out_shape=[jax.ShapeDtypeStruct(r.shape, r.dtype) fo...  5.72 us

profile of v3, /device:TPU:1, one launch (start us, length us, event | category | flops | bytes accessed | tf_op | source)
XLA Modules:
  0.0 139.0 jit_solution(9020929538792950893)
XLA Ops:
  0.6 125.5 %shard_map.102 = (bf16[48,2048]{1,0:T(8,128)(2,1)}, bf16[48,3328]{1,0:T(8,128)(2,1)}, bf16[3328,1024]{1,0:T(8,128)(2,1)}, bf16[1024,2048]{1,0:T(8,128)(2,1)}) custom-call(f32[1,48]{1,0:T(1,128)} %bitcast.3, s32[1,48]{1,0:T(1,128)} %bitcast.4, s32[1,48]{1,0:T(1,128)} %bitcast.5, bf16[48,3328]{1,0:T(8,128)(2,1)} %hid_ref.1, bf16[3328,1024]{1,0:T(8,128)(2,1)} %wd_ref.1, ...), custom_call_target="tpu_custom_call" | custom-call | flops 25367150592 | bytes 22020096 | tf_op jit(solution)/shard_map/pallas_call | solution.py:515
  126.1 0.0 copy-start
  126.1 2.9 %copy-done = bf16[3328,1024]{1,0:T(8,128)(2,1)S(1)} copy-done((bf16[3328,1024]{1,0:T(8,128)(2,1)S(1)}, bf16[3328,1024]{1,0:T(8,128)(2,1)}, u32[]{:S(2)}) %copy-start) | copy-done | bytes 6815768
  129.0 0.0 copy-start.1
  129.0 2.2 %copy-done.1 = bf16[1024,2048]{1,0:T(8,128)(2,1)S(1)} copy-done((bf16[1024,2048]{1,0:T(8,128)(2,1)S(1)}, bf16[1024,2048]{1,0:T(8,128)(2,1)}, u32[]{:S(2)}) %copy-start.1) | copy-done | bytes 4194328
  131.2 0.0 copy-start.2
  131.2 1.0 copy-done.2
  132.2 0.0 copy-start.3
  132.2 0.9 copy-done.3
  133.1 5.7 %shard_map.103 = (bf16[48,2048]{1,0:T(8,128)(2,1)}, bf16[48,3328]{1,0:T(8,128)(2,1)}, bf16[3328,1024]{1,0:T(8,128)(2,1)}, bf16[1024,2048]{1,0:T(8,128)(2,1)}) custom-call(bf16[48,2048]{1,0:T(8,128)(2,1)S(1)} %copy-done.3, bf16[48,3328]{1,0:T(8,128)(2,1)S(1)} %copy-done.2, bf16[3328,1024]{1,0:T(8,128)(2,1)S(1)} %copy-done, bf16[1024,2048]{1,0:T(8,128)(2,1)S(1)} %copy-done.1), custom_call_target="tpu_custom_call" | custom-call | bytes 22020096 | tf_op jit(solution)/shard_map/pallas_call | solution.py:558
Async XLA Ops:
  126.1 2.9 %copy-start = (bf16[3328,1024]{1,0:T(8,128)(2,1)S(1)}, bf16[3328,1024]{1,0:T(8,128)(2,1)}, u32[]{:S(2)}) copy-start(bf16[3328,1024]{1,0:T(8,128)(2,1)} %get-tuple-element.10.refs_2_) | copy-start | bytes 20447236
  129.0 2.2 %copy-start.1 = (bf16[1024,2048]{1,0:T(8,128)(2,1)S(1)}, bf16[1024,2048]{1,0:T(8,128)(2,1)}, u32[]{:S(2)}) copy-start(bf16[1024,2048]{1,0:T(8,128)(2,1)} %get-tuple-element.11.refs_3_) | copy-start | bytes 12582916
  131.2 1.0 copy-start.2
  132.2 0.9 copy-start.3

commit v4 on v3

--- a/solution.py
+++ b/solution.py
@@ -201,8 +201,12 @@
             self.swaps, self.moves, self.spread, self.relays = {}, {}, {}, {}
 
         def fill(self, j, which, ref):
-            value = self.term(pl.multiple_of(which * half1 + j * 256, 256))
-            ref[j] = value.reshape(4, quarter, 256)
+            for n in range(half1 // 256):
+                value = self.term(self.base(j), pl.multiple_of(which * half1 + n * 256, 256))
+                ref[j, :, :, n * 256:(n + 1) * 256] = value.reshape(4, quarter // 2, 256)
+
+        def base(self, j):
+            return 2 * (1 - j)
 
         def theirs(self, j):
             self.fill(j, 1 - core, sib_out)
@@ -231,25 +235,24 @@
             total = part[j, x]
             for d in range(3):
                 total = total + xin[j, d].astype(F32)
-            cols = slice(j * 256, j * 256 + 256)
-            self.dest[core, x, :, cols] = total.astype(BF)
-            spot = self.dest.at[core, x, :, pl.ds(j * 256, 256)]
+            self.dest[core, self.base(j) + x // 2, x % 2] = total.astype(BF)
+            spot = self.dest.at[core, self.base(j) + x // 2, x % 2]
             self.spread[j] = [send(spot, spot, dx=d) for d in near]
 
         def relay(self, j):
             arrive(self.spread[j])
-            spot = self.dest.at[core, :, :, pl.ds(j * 256, 256)]
+            spot = self.dest.at[core, pl.ds(self.base(j), 2)]
             self.relays[j] = send(spot, spot, dc=1)
 
         def done(self, j):
             arrive([self.relays[j]])
             finish(self.moves[j])
 
-    def back_term(start):
-        return dot_nt(cot[...].reshape(tokens, -1), wo[pl.ds(start, 256), :])
-
-    def down_term(start):
-        return dot_nn(hid[...].reshape(tokens, -1), wd[:, pl.ds(start, 256)])
+    def back_term(base, start):
+        return dot_nt(cot[base:base + 2].reshape(tokens // 2, -1), wo[pl.ds(start, 256), :])
+
+    def down_term(base, start):
+        return dot_nn(hid[base:base + 2].reshape(tokens // 2, -1), wd[:, pl.ds(start, 256)])
 
     sum_back, sum_down = Reduce(back_term, gm), Reduce(down_term, dn)
 
@@ -267,27 +270,23 @@
     hidden_rows.hand_across(0)
     sum_back.mine(1)
     sum_back.start(1)
+    sum_back.sum(0)
+    sum_back.sum(1)
     hidden_rows.hand_across(2)
-    sum_back.sum(0)
+    sum_back.relay(0)
     loads[3].wait()
-    sum_back.sum(1)
-    sum_back.relay(0)
-    hidden_rows.done()
-    sum_down.theirs(0)
     sum_back.done(0)
-    sum_down.swap(0)
-    sum_back.relay(1)
-    sum_down.mine(0)
-    sum_back.done(1)
-
-    def block_rows(full, axis, d):
+
+    def block_rows(full, axis, d, group):
         out = []
         for h in range(2):
             if axis == "z":
-                out.append(full[h, d])
+                out.append(full[h, d].reshape(quarter, half1))
             else:
+                places = range(4) if group is None else range(2 * group, 2 * group + 2)
+                first = d % 2 * rows
                 out.append(
-                    jnp.concatenate([full[h, i, d * rows:(d + 1) * rows] for i in range(4)], axis=0)
+                    jnp.concatenate([full[h, i, d // 2, first:first + rows] for i in places], axis=0)
                 )
         return out
 
@@ -303,32 +302,39 @@
         def axis(self, s, stage):
             return "zy"[(s + stage) % 2]
 
-        def term(self, s, stage, d, part):
+        def term(self, s, stage, d, part, group=None):
             if stage == 0:
-                return self.mult(s, block_rows(self.full, self.axis(s, 0), d), part)
+                return self.mult(s, block_rows(self.full, self.axis(s, 0), d, group), part)
             return self.acc[s, d * rows:(d + 1) * rows, part]
 
-        def move(self, key, s, stage, d, part, value, dst, sign):
+        def move(self, key, s, stage, d, part, value, dst, sign, group=None):
             out = self.stages[stage][0]
             cols = pl.ds(part.start, part.stop - part.start)
-            out[s, d - 1, :, part] = value.astype(BF)
-            self.got[key, s, stage, sign] = send(
-                out.at[s, d - 1, :, cols], dst.at[:, cols], **{"d" + self.axis(s, stage): sign}
+            count = value.shape[0]
+            first = 0 if group is None else group * count
+            out[s, d - 1, first:first + count, part] = value.astype(BF)
+            lines = pl.ds(first, count)
+            copy = send(
+                out.at[s, d - 1, lines, cols], dst.at[lines, cols], **{"d" + self.axis(s, stage): sign}
             )
+            self.got.setdefault((key, s, stage, sign), []).append(copy)
 
         def take(self, key, s, stage, sign):
-            arrive([self.got.pop((key, s, stage, sign))])
-
-        def far(self, s, stage):
+            arrive(self.got.pop((key, s, stage, sign)))
+
+        def far(self, s, stage, group=None):
             relay = self.stages[stage][1]
             for part, sign in zip(self.parts, (1, -1)):
-                self.move("relay", s, stage, 2, part, self.term(s, stage, 2, part), relay.at[s], sign)
-
-        def direct(self, s, stage):
+                value = self.term(s, stage, 2, part, group)
+                self.move("relay", s, stage, 2, part, value, relay.at[s], sign, group)
+
+        def direct(self, s, stage, signs=(1, -1), group=None):
             inn = self.stages[stage][2]
             for part, sign in zip(self.parts[::-1], (1, -1)):
-                d = sign % 4
-                self.move("direct", s, stage, d, part, self.term(s, stage, d, part), inn.at[s, d // 2], sign)
+                if sign in signs:
+                    d = sign % 4
+                    value = self.term(s, stage, d, part, group)
+                    self.move("direct", s, stage, d, part, value, inn.at[s, d // 2], sign, group)
 
         def joined(self, s, stage):
             relay, inn = self.stages[stage][1:]
@@ -396,7 +402,7 @@
             return 0
 
         lax.fori_loop(first, last, body, 0)
-        for i in (last - 2, last - 1):
+        for i in range(max(first, last - 2), last):
             out_copy(i, i % 2).wait()
 
     def hid_cols(i):
@@ -410,7 +416,7 @@
     per = half1 // 256
 
     def dn_cols(i):
-        return dn[i // per, :, :, pl.ds(pl.multiple_of((i % per) * 256, 256), 256)].reshape(tokens, 256)
+        return dn[i // per, :, :, :, pl.ds(pl.multiple_of((i % per) * 256, 256), 256)].reshape(tokens, 256)
 
     def times_cot(left):
         return dot_nn(left, cot[...].reshape(tokens, d2))
@@ -421,13 +427,20 @@
     def out_rows(first, last):
         weight_rows(dn_cols, times_cot, go_ref, first, last)
 
+    grad_hidden.far(0, 0)
+    grad_hidden.far(1, 0, group=1)
+    sum_back.relay(1)
+    hidden_rows.done()
+    sum_down.theirs(0)
+    sum_down.swap(0)
+    sum_back.done(1)
+    sum_down.mine(0)
     sum_down.start(0)
-    for s in (0, 1):
-        grad_hidden.far(s, 0)
     sum_down.theirs(1)
     sum_down.swap(1)
     sum_down.mine(1)
     sum_down.start(1)
+    grad_hidden.far(1, 0, group=0)
     for s in (0, 1):
         grad_hidden.direct(s, 0)
     sum_down.sum(0)
@@ -436,9 +449,8 @@
     sum_down.sum(1)
     for s in (0, 1):
         grad_hidden.own(s)
-    down_rows(0, 2)
     sum_down.relay(0)
-    down_rows(2, 4)
+    down_rows(0, 4)
     sum_down.relay(1)
     sum_down.done(0)
     sum_down.done(1)
@@ -446,19 +458,19 @@
         projected.far(s, 0)
     for s in (0, 1):
         projected.direct(s, 0)
-    down_rows(4, 6)
     for s in (0, 1):
         grad_hidden.total(s)
         grad_hidden.far(s, 1)
     for s in (0, 1):
         grad_hidden.direct(s, 1)
+    down_rows(4, 7)
     for s in (0, 1):
         projected.joined(s, 0)
     for s in (0, 1):
         grad_hidden.joined(s, 1)
     for s in (0, 1):
         projected.own(s)
-    down_rows(6, hid_blocks)
+    down_rows(7, hid_blocks)
     g_done = grad_hidden.last(gh_ref, lsem.at[4])
     out_rows(0, 2)
     for s in (0, 1):
@@ -466,9 +478,10 @@
         projected.far(s, 1)
     for s in (0, 1):
         projected.direct(s, 1)
+    out_rows(2, 3)
     for s in (0, 1):
         projected.joined(s, 1)
-    out_rows(2, d1 // 256)
+    out_rows(3, d1 // 256)
     p_done = projected.last(proj_ref, lsem.at[5])
     g_done.wait()
     p_done.wait()
@@ -529,13 +542,13 @@
             pltpu.VMEM((4, 4, rows, d2), BF),
             pltpu.VMEM((4, 4, rows, d2), BF),
             pltpu.VMEM((4, 4, 8, 128), F32),
-            pltpu.VMEM((2, 4, quarter, 256), F32),
-            pltpu.VMEM((2, 4, quarter, 256), F32),
-            pltpu.VMEM((2, 4, quarter, 256), F32),
-            pltpu.VMEM((2, 4, quarter, 256), BF),
-            pltpu.VMEM((2, 3, quarter, 256), BF),
-            pltpu.VMEM((2, 4, quarter, half1), BF),
-            pltpu.VMEM((2, 4, quarter, half1), BF),
+            pltpu.VMEM((2, 4, quarter // 2, half1), F32),
+            pltpu.VMEM((2, 4, quarter // 2, half1), F32),
+            pltpu.VMEM((2, 4, quarter // 2, half1), F32),
+            pltpu.VMEM((2, 4, quarter // 2, half1), BF),
+            pltpu.VMEM((2, 3, quarter // 2, half1), BF),
+            pltpu.VMEM((2, 4, 2, quarter // 2, half1), BF),
+            pltpu.VMEM((2, 4, 2, quarter // 2, half1), BF),
             *reduce_shapes(ff),
             *reduce_shapes(d2),
             pltpu.VMEM((2, 256, d2), BF),
@@ -562,7 +575,7 @@
         out_specs=[anywhere] * 4,
         scratch_shapes=[pltpu.VMEM(r.shape, r.dtype) for r in results]
         + [pltpu.SemaphoreType.DMA((24,)), pltpu.SemaphoreType.DMA((24,))],
-        compiler_params=pltpu.CompilerParams(vmem_limit_bytes=32 << 20),
+        compiler_params=pltpu.CompilerParams(vmem_limit_bytes=60 << 20),
         cost_estimate=pl.CostEstimate(
             flops=0, bytes_accessed=4 * d1 * (ff + d2), transcendentals=0
         ),

time: 139 us -> 132 us (0.950)
  local copies, waits for them, and re-layouts: 7.01 us -> 0 us
    unnamed x8 -> x0, local copies, waits for them, and re-layouts: 7.01 us -> none
    pallas_call x1, Pallas kernels: 125 us -> 121 us  [local(): pl.pallas_call(functools.partial(kernel, rows), out_shape=(jax.ShapeDtype...]
    pallas_call x1, Pallas kernels: 5.72 us -> 8.67 us  [local(): pl.pallas_call(keep, out_shape=[jax.ShapeDtypeStruct(r.shape, r.dtype) fo...]
where the time goes in v4:
time: 132 us; the launch traced here: 131 us
  Pallas kernels  130 us (98%)
    pallas_call x1, Pallas kernels, local(): pl.pallas_call(functools.partial(kernel, rows), out_shape=(jax.ShapeDtype...  121 us
    pallas_call x1, Pallas kernels, local(): pl.pallas_call(keep, out_shape=[jax.ShapeDtypeStruct(r.shape, r.dtype) fo...  8.67 us

profile of v4, /device:TPU:1, one launch (start us, length us, event | category | flops | bytes accessed | tf_op | source)
XLA Modules:
  0.0 130.9 jit_solution(4277131199524748789)
XLA Ops:
  0.6 121.5 %shard_map.102 = (bf16[48,2048]{1,0:T(8,128)(2,1)}, bf16[48,3328]{1,0:T(8,128)(2,1)}, bf16[3328,1024]{1,0:T(8,128)(2,1)}, bf16[1024,2048]{1,0:T(8,128)(2,1)}) custom-call(f32[1,48]{1,0:T(1,128)} %bitcast.3, s32[1,48]{1,0:T(1,128)} %bitcast.4, s32[1,48]{1,0:T(1,128)} %bitcast.5, bf16[48,3328]{1,0:T(8,128)(2,1)} %hid_ref.1, bf16[3328,1024]{1,0:T(8,128)(2,1)} %wd_ref.1, ...), custom_call_target="tpu_custom_call" | custom-call | flops 25367150592 | bytes 22020096 | tf_op jit(solution)/shard_map/pallas_call | solution.py:528
  122.1 8.7 %shard_map.103 = (bf16[48,2048]{1,0:T(8,128)(2,1)}, bf16[48,3328]{1,0:T(8,128)(2,1)}, bf16[3328,1024]{1,0:T(8,128)(2,1)}, bf16[1024,2048]{1,0:T(8,128)(2,1)}) custom-call(bf16[48,2048]{1,0:T(8,128)(2,1)} %get-tuple-element.8.refs_0_, bf16[48,3328]{1,0:T(8,128)(2,1)} %get-tuple-element.9.refs_1_, bf16[3328,1024]{1,0:T(8,128)(2,1)} %get-tuple-element.10.refs_2_, ...), custom_call_target="tpu_custom_call" | custom-call | bytes 22020096 | tf_op jit(solution)/shard_map/pallas_call | solution.py:571

commit v5 on v4

--- a/solution.py
+++ b/solution.py
@@ -67,7 +67,7 @@
         pltpu.make_async_copy(wo_ref, wo, lsem.at[2]),
         pltpu.make_async_copy(wd_ref, wd, lsem.at[3]),
     ]
-    for load in loads:
+    for load in loads[:2]:
         load.start()
 
     sign = ((segment_ref[...] & 1) * (1 - 2 * (slot_ref[...] & 1))).astype(F32)
@@ -83,6 +83,8 @@
     pl.semaphore_wait(barrier, len(peers))
     for load in loads[:2]:
         load.wait()
+    for load in loads[2:]:
+        load.start()
 
     class Gather:
         def __init__(self, full):
@@ -183,11 +185,21 @@
     )
     weight = -beta_scale * jax.nn.sigmoid(-beta_scale * margin)
 
-    def scale(i, _):
-        tile = tiles[i // 4, i % 4]
+    def scale(q, p):
+        tile = tiles[q, p]
         line = jnp.sum(jnp.where(tile[1:2] == pairs, weight, 0.0), axis=0, keepdims=True) * tile[2:3]
         coef = jnp.broadcast_to(line, (8, 128)).T[0:rows, 0:1]
-        cot[i // 4, i % 4] = (coef * hg[i // 4, i % 4].astype(F32)).astype(BF)
+        cot[q, p] = (coef * hg[q, p].astype(F32)).astype(BF)
+
+    def scale_near(i, _):
+        q, p = i // 3, i % 3
+        scale(q + q // 2, p + p // 2)
+        return 0
+
+    def scale_far(i, _):
+        other = lax.max(i - 4, 0)
+        across = lax.min(i // 4, 1)
+        scale(2 + across * (other + other // 2 - 2), i + across * (2 - i))
         return 0
 
     tokens = 16 * rows
@@ -256,9 +268,10 @@
 
     sum_back, sum_down = Reduce(back_term, gm), Reduce(down_term, dn)
 
+    lax.fori_loop(0, 9, scale_near, 0)
     grad_rows.done()
     hidden_rows.hand_on()
-    lax.fori_loop(0, 16, scale, 0)
+    lax.fori_loop(0, 7, scale_far, 0)
     loads[2].wait()
     sum_back.theirs(0)
     sum_back.swap(0)
@@ -345,6 +358,13 @@
                 value = value + relay[s, :, part].astype(F32)
                 self.move("joined", s, stage, d, part, value, inn.at[s, d // 2], sign)
 
+        def straight(self, s):
+            out, relay, inn = self.stages[1]
+            for d, dst in ((2, relay.at[s]), (1, inn.at[s, 0]), (3, inn.at[s, 1])):
+                out[s, d - 1] = self.acc[s, d * rows:(d + 1) * rows].astype(BF)
+                copy = send(out.at[s, d - 1], dst, **{"d" + self.axis(s, 1): d})
+                self.got.setdefault(("straight", s), []).append(copy)
+
         def own(self, s):
             for part in self.parts:
                 self.acc[s, :, part] = self.term(s, 0, 0, part)
@@ -359,10 +379,15 @@
         def last(self, ref, sem):
             inn = self.stages[1][2]
             for s in (0, 1):
-                for key in ("direct", "joined"):
-                    for sign in (1, -1):
-                        self.take(key, s, 1, sign)
-                value = self.acc[s, 0:rows] + inn[s, 0].astype(F32) + inn[s, 1].astype(F32)
+                value = self.acc[s, 0:rows]
+                if ("straight", s) in self.got:
+                    arrive(self.got.pop(("straight", s)))
+                    value = value + self.stages[1][1][s].astype(F32)
+                else:
+                    for key in ("direct", "joined"):
+                        for sign in (1, -1):
+                            self.take(key, s, 1, sign)
+                value = value + inn[s, 0].astype(F32) + inn[s, 1].astype(F32)
                 self.fin[:, s * self.width:(s + 1) * self.width] = value.astype(BF)
             copy = pltpu.make_async_copy(self.fin, ref, sem)
             copy.start()
@@ -472,16 +497,10 @@
         projected.own(s)
     down_rows(7, hid_blocks)
     g_done = grad_hidden.last(gh_ref, lsem.at[4])
-    out_rows(0, 2)
     for s in (0, 1):
         projected.total(s)
-        projected.far(s, 1)
-    for s in (0, 1):
-        projected.direct(s, 1)
-    out_rows(2, 3)
-    for s in (0, 1):
-        projected.joined(s, 1)
-    out_rows(3, d1 // 256)
+        projected.straight(s)
+    out_rows(0, d1 // 256)
     p_done = projected.last(proj_ref, lsem.at[5])
     g_done.wait()
     p_done.wait()

time: 132 us -> 128 us (0.970)
  Pallas kernels: 130 us -> 127 us
    pallas_call x1, Pallas kernels: 121 us -> 118 us  [local(): pl.pallas_call(functools.partial(kernel, rows), out_shape=(jax.ShapeDtype...]
where the time goes in v5:
time: 128 us; the launch traced here: 127 us
  Pallas kernels  127 us (99%)
    pallas_call x1, Pallas kernels, local(): pl.pallas_call(functools.partial(kernel, rows), out_shape=(jax.ShapeDtype...  118 us
    pallas_call x1, Pallas kernels, local(): pl.pallas_call(keep, out_shape=[jax.ShapeDtypeStruct(r.shape, r.dtype) fo...  8.67 us

profile of v5, /device:TPU:1, one launch (start us, length us, event | category | flops | bytes accessed | tf_op | source)
XLA Modules:
  0.0 127.5 jit_solution(13292431591558212680)
XLA Ops:
  0.6 118.0 %shard_map.102 = (bf16[48,2048]{1,0:T(8,128)(2,1)}, bf16[48,3328]{1,0:T(8,128)(2,1)}, bf16[3328,1024]{1,0:T(8,128)(2,1)}, bf16[1024,2048]{1,0:T(8,128)(2,1)}) custom-call(f32[1,48]{1,0:T(1,128)} %bitcast.3, s32[1,48]{1,0:T(1,128)} %bitcast.4, s32[1,48]{1,0:T(1,128)} %bitcast.5, bf16[48,3328]{1,0:T(8,128)(2,1)} %hid_ref.1, bf16[3328,1024]{1,0:T(8,128)(2,1)} %wd_ref.1, ...), custom_call_target="tpu_custom_call" | custom-call | flops 25367150592 | bytes 22020096 | tf_op jit(solution)/shard_map/pallas_call | solution.py:547
  118.6 8.7 %shard_map.103 = (bf16[48,2048]{1,0:T(8,128)(2,1)}, bf16[48,3328]{1,0:T(8,128)(2,1)}, bf16[3328,1024]{1,0:T(8,128)(2,1)}, bf16[1024,2048]{1,0:T(8,128)(2,1)}) custom-call(bf16[48,2048]{1,0:T(8,128)(2,1)} %get-tuple-element.8.refs_0_, bf16[48,3328]{1,0:T(8,128)(2,1)} %get-tuple-element.9.refs_1_, bf16[3328,1024]{1,0:T(8,128)(2,1)} %get-tuple-element.10.refs_2_, ...), custom_call_target="tpu_custom_call" | custom-call | bytes 22020096 | tf_op jit(solution)/shard_map/pallas_call | solution.py:590
